TPU v7x, 32 devices: a whole 2x2x4 slice. The times are simulated.
32 devices in a mesh: seq: 16 (over z, y, core), req: 2 (over x).
Axes of the slice: x: 2, y: 2, z: 4, core: 2. Of those that a mesh axis runs over, the one named last changes fastest.
Arguments:
- hidden_in: bfloat16 [32, 4, 2048], P('req'), may hold values from -6 to 6
- attn_gain: float32 [2048], replicated, may hold values from 0.5 to 1.5
- q_gain: float32 [256], replicated, may hold values from 0.5 to 1.5
- k_gain: float32 [256], replicated, may hold values from 0.5 to 1.5
- post_attn_gain: float32 [2048], replicated, may hold values from 0.5 to 1.5
- ffn_gain: float32 [2048], replicated, may hold values from 0.5 to 1.5
- post_ffn_gain: float32 [2048], replicated, may hold values from 0.5 to 1.5
- w_qkv: bfloat16 [2048, 3072], P('seq', 'req'), may hold values from -0.125 to 0.125
- w_out: bfloat16 [2048, 2048], P('seq', 'req'), may hold values from -0.125 to 0.125
- w_gate: bfloat16 [2048, 8192], P('req', 'seq'), may hold values from -0.125 to 0.125
- w_up: bfloat16 [2048, 8192], P('req', 'seq'), may hold values from -0.125 to 0.125
- w_down: bfloat16 [8192, 2048], P('seq', 'req'), may hold values from -0.0625 to 0.0625
- prompt_keys: bfloat16 [4, 2048, 512], P('req', 'seq')
- prompt_values: bfloat16 [4, 2048, 512], P('req', 'seq'), may hold values from -6 to 6
- tail_keys: bfloat16 [2, 4096, 512], P('req', 'seq')
- tail_values: bfloat16 [2, 4096, 512], P('req', 'seq'), may hold values from -6 to 6
- group_of: int32 [32], P('req'), may hold values from 0 to 3, as said below
- prompt_lengths: int32 [4], P('req'), may hold values from 1 to 2048
- tail_lengths: int32 [32], P('req'), may hold values from 1 to 256
- page_table: int32 [2, 256], P('req'), may hold values from 0 to 255, each once within a row
Outputs:
- layer_out: bfloat16 [32, 4, 2048], P('req')
Inputs may be any that keep to these rules, and one draw needn't show every extreme that they name: `group_of`: request i belongs to one of the 2 groups i // 16 * 2 to i // 16 * 2 + 1 of its own block of requests. `page_table`: each row lists every pool page of its index of req once; entry j * 16 + p is the pool page of page p of the j-th request of that block.
All inputs are finite; a program needn't handle non-finite values.
Results may differ from a plain program's by a relative error of at most 0.012.
The roundings to bfloat16 on the way count: a program that leaves them out, or rounds other values in their place, can miss the bound.
Values may be sent and summed in bfloat16 or wider, within the bound.
No kernel may reach another device: no remote copies, remote signals or barrier semaphores. Data moves between devices by JAX's collectives and lax.ppermute only.
A program may use at most 128 MiB of HBM per device.

v0:
```python
import functools

import jax
import jax.numpy as jnp
from jax import lax
from jax.experimental import pallas as pl
from jax.experimental.pallas import tpu as pltpu
from jax.sharding import PartitionSpec as P

D = 2048
H = 8
KV = 2
HD = 256
PAGE = 16
QKV = 3072


EPSILON = 1e-06
NEGATIVE = -1e30
LINK_SCALE = 512.0


def normalize(values):
    return values * lax.rsqrt(jnp.mean(values * values, axis=-1, keepdims=True) + EPSILON)


def split_three(values):
    high = values.astype(jnp.bfloat16)
    rest = values - high.astype(jnp.float32)
    middle = rest.astype(jnp.bfloat16)
    low = (rest - middle.astype(jnp.float32)).astype(jnp.bfloat16)
    return jnp.stack([high, middle, low])


def exchange(blocks, axes, groups=None):
    return lax.all_to_all(
        blocks, axes, split_axis=0, concat_axis=0, tiled=True, axis_index_groups=groups
    )


def tie(*arrays):
    return lax.optimization_barrier(arrays)


def spread(block, copies):
    return jnp.broadcast_to(block[None], (copies,) + block.shape)


def gather_rows(rows, count):
    return exchange(spread(rows, count), "seq").reshape(count * rows.shape[0], rows.shape[1])


def call(
    kernel, name, out_shape, *operands, scratch=(), hbm_from=None, out_space=pltpu.VMEM, limit=16
):
    in_specs = [pl.BlockSpec(memory_space=pltpu.SMEM)]
    for i in range(1, len(operands)):
        space = pltpu.HBM if hbm_from is not None and i >= hbm_from else pltpu.VMEM
        in_specs.append(pl.BlockSpec(memory_space=space))
    return pl.pallas_call(
        kernel,
        name=name,
        out_shape=out_shape,
        in_specs=in_specs,
        out_specs=jax.tree.map(lambda _: pl.BlockSpec(memory_space=out_space), out_shape),
        scratch_shapes=scratch,
        compiler_params=pltpu.CompilerParams(vmem_limit_bytes=limit * 1024 * 1024),
    )(*operands)


def norm_columns_kernel(where_ref, hidden_ref, gain_ref, out_ref):
    columns = out_ref.shape[1]
    hidden = hidden_ref[...].astype(jnp.float32)
    scale = lax.rsqrt(jnp.mean(hidden * hidden, axis=-1, keepdims=True) + EPSILON)
    cols = pl.ds(pl.multiple_of(where_ref[0] * columns, columns), columns)
    normed = hidden_ref[:, :, cols].astype(jnp.float32) * scale * gain_ref[:, cols]
    out_ref[...] = normed.reshape(out_ref.shape).astype(jnp.bfloat16)


def head_norm_kernel(where_ref, projected_ref, gains_ref, q_ref, k_ref, v_ref):
    width = projected_ref.shape[2]
    copies, rows, _ = q_ref.shape
    fill = jnp.zeros((k_ref.shape[0] - rows, HD), jnp.float32)
    for head in range(H + 2 * KV):
        half, first = divmod(head * HD, width)
        values = normalize(projected_ref[half, :, first : first + HD])
        if head < H:
            values = (values * gains_ref[0:1, :]).astype(jnp.bfloat16)
            for i in range(copies):
                q_ref[i, :, head * HD : (head + 1) * HD] = values
        else:
            if head < H + KV:
                values = values * gains_ref[1:2, :]
            values = values.astype(jnp.bfloat16).astype(jnp.float32)
            target, slot = (k_ref, head - H) if head < H + KV else (v_ref, head - H - KV)
            target[:, slot * HD : (slot + 1) * HD] = jnp.concatenate([values, fill])


def dot_last(a, b):
    return lax.dot_general(a, b, (((1,), (1,)), ((), ())), preferred_element_type=jnp.float32)


def block_kernel(
    step_count,
    where_ref,
    q_ref,
    live_ref,
    new_k_ref,
    new_v_ref,
    keys_ref,
    values_ref,
    out_ref,
):
    copies, steps, _ = q_ref.shape
    tokens = copies * steps
    columns = out_ref.shape[2]
    group = H // KV
    queries = q_ref[...].reshape(tokens, H * HD)
    live = jnp.concatenate([live_ref[...]] * group) > 0.5
    first_token = where_ref[0] * step_count
    shape = (group * tokens, new_k_ref.shape[0])
    step = lax.broadcasted_iota(jnp.int32, shape, 0) % tokens - first_token
    new_index = lax.broadcasted_iota(jnp.int32, shape, 1)
    new_live = (step >= new_index) & (step < step_count)
    for kv in range(KV):
        span = slice(kv * HD, (kv + 1) * HD)
        q = jnp.concatenate(
            [queries[:, (kv * group + g) * HD : (kv * group + g + 1) * HD] for g in range(group)]
        )
        scores = jnp.where(live, dot_last(q, keys_ref[:, span]), NEGATIVE)
        top = jnp.max(scores, axis=1, keepdims=True)
        probs = jnp.where(live, jnp.exp(scores - top), 0.0)
        total = jnp.sum(probs, axis=1, keepdims=True)
        accum = jnp.dot(
            probs.astype(jnp.bfloat16), values_ref[:, span], preferred_element_type=jnp.float32
        )
        new_scores = dot_last(q, new_k_ref[:, span].astype(jnp.bfloat16))
        new_scores = jnp.where(new_live, new_scores, NEGATIVE)
        both = jnp.maximum(top, jnp.max(new_scores, axis=1, keepdims=True))
        carried = jnp.exp(top - both)
        new_probs = jnp.where(new_live, jnp.exp(new_scores - both), 0.0)
        total = total * carried + jnp.sum(new_probs, axis=1, keepdims=True)
        accum = accum * carried
        for u in range(step_count):
            accum = accum + new_probs[:, u : u + 1] * new_v_ref[u : u + 1, span]
        sent = accum.astype(jnp.bfloat16)
        parts = []
        for value in (both, total):
            for _ in range(3):
                part = value.astype(jnp.bfloat16).astype(jnp.float32)
                parts.append(part)
                value = value - part
        lane = lax.broadcasted_iota(jnp.int32, (group * tokens, 128), 1)
        wide = jnp.zeros((group * tokens, 128), jnp.float32)
        for i, part in enumerate(parts):
            wide = jnp.where(lane == i, part, wide)
        turned = jnp.transpose(wide)[:16].astype(jnp.bfloat16)
        for g in range(group):
            pair = turned[:, g // 2 * 128 : (g // 2 + 1) * 128]
            for part in range(HD // columns):
                target = (kv * group + g) * (HD // columns) + part
                out_ref[target, :tokens, :] = sent[
                    g * tokens : (g + 1) * tokens, part * columns : (part + 1) * columns
                ]
                out_ref[target, tokens:, :] = pair


def out_kernel(req_count, where_ref, got_ref, *refs):
    w_refs = refs[:req_count]
    out_ref, turned_ref = refs[req_count:]
    blocks = got_ref.shape[0]
    copies, steps, _ = out_ref.shape
    tokens = copies * steps
    columns = got_ref.shape[2]
    head = where_ref[0] * columns // HD
    stats = got_ref[:, tokens:, :].astype(jnp.float32)
    tops = stats[:, 0, :] + stats[:, 1, :] + stats[:, 2, :]
    totals = stats[:, 3, :] + stats[:, 4, :] + stats[:, 5, :]
    rest = jnp.zeros((128 - 2 * blocks, 128), jnp.float32)
    turned_ref[...] = jnp.transpose(jnp.concatenate([tops, totals, rest]))
    mine = turned_ref[pl.ds(pl.multiple_of(head % 2 * tokens, tokens), tokens), :]
    tops = mine[:, :blocks]
    highest = jnp.max(tops, axis=1, keepdims=True)
    weights = jnp.exp(tops - highest)
    denominator = jnp.sum(mine[:, blocks : 2 * blocks] * weights, axis=1, keepdims=True)
    numerator = jnp.zeros((tokens, columns), jnp.float32)
    for b in range(blocks):
        numerator = numerator + got_ref[b, :tokens, :].astype(jnp.float32) * weights[:, b : b + 1]
    attention = (numerator / denominator).astype(jnp.bfloat16)
    for j, w_ref in enumerate(w_refs):
        width = w_ref.shape[1]
        part = jnp.dot(attention, w_ref[...], preferred_element_type=jnp.float32)
        part = part.astype(jnp.bfloat16)
        for i in range(copies):
            out_ref[i, :, j * width : (j + 1) * width] = part[i * steps : (i + 1) * steps]


def summed(req_count, where_ref, got_ref):
    width = got_ref.shape[2] // req_count
    blocks = []
    for i in range(req_count):
        j = lax.rem(where_ref[1] - i + req_count, req_count)
        cols = pl.ds(pl.multiple_of(j * width, width), width)
        blocks.append(jnp.sum(got_ref[:, :, cols].astype(jnp.float32), axis=0))
    return jnp.concatenate(blocks, axis=1)


def residual_kernel(
    req_count, where_ref, got_ref, hidden_ref, post_gain_ref, ffn_gain_ref, out_ref, residual_ref
):
    attn_out = summed(req_count, where_ref, got_ref)
    hidden = hidden_ref[where_ref[0]].astype(jnp.float32)
    residual = hidden + normalize(attn_out) * post_gain_ref[...]
    residual_ref[...] = residual
    ffn_in = (normalize(residual) * ffn_gain_ref[...]).astype(jnp.bfloat16)
    for i in range(out_ref.shape[0]):
        out_ref[i] = ffn_in


def last_kernel(req_count, where_ref, got_ref, residual_ref, gain_ref, out_ref):
    down_out = summed(req_count, where_ref, got_ref)
    layer = (residual_ref[...] + normalize(down_out) * gain_ref[...]).astype(jnp.bfloat16)
    for i in range(out_ref.shape[0]):
        out_ref[i] = layer


def start_copies(moves, sem_ref):
    copies = [
        pltpu.make_async_copy(source, target, sem_ref.at[i])
        for i, (source, target) in enumerate(moves)
    ]
    for copy in copies:
        copy.start()
    return copies


def chunks_of(rows):
    size = min(rows, 256)
    return [(first, size) for first in range(0, rows, size)]


def x_columns(x_ref, where_ref, req_count, j, rows):
    start = lax.rem(where_ref[1] - j + req_count, req_count) * rows
    return x_ref.at[:, :, pl.ds(pl.multiple_of(start, rows), rows)]


def chunked_dot(x, held, chunks, waits):
    total = None
    for first, size in chunks:
        next(waits).wait()
        part = jnp.dot(
            x[:, first : first + size],
            held[first : first + size, :],
            preferred_element_type=jnp.float32,
        )
        total = part if total is None else total + part
    return total


def own_kernel(req_count, where_ref, x_ref, gate_ref, up_ref, out_ref, x_held, held, sem_ref):
    rows = gate_ref.shape[0]
    chunks = chunks_of(rows)
    moves = [(x_columns(x_ref, where_ref, req_count, 0, rows), x_held)]
    for i, w_ref in enumerate((gate_ref, up_ref)):
        for first, size in chunks:
            span = pl.ds(first, size)
            moves.append((w_ref.at[span, :], held.at[i, span, :]))
    waits = iter(start_copies(moves, sem_ref))
    blocks, steps, _ = x_held.shape
    next(waits).wait()
    x = x_held[...].reshape(blocks * steps, rows)
    for i in range(2):
        out_ref[i] = chunked_dot(x, held.at[i], chunks, waits)


def ffn_kernel(req_count, gate_rows, where_ref, x_ref, own_ref, down_ref, *refs):
    others = req_count - 1
    packed_refs = refs[:others]
    out_ref, x_held, own_held, downs, parts_ref, held, sem_ref = refs[others:]
    down_rows, width = downs.shape[1:]
    piece_count = down_ref.shape[1] // width
    chunks = chunks_of(gate_rows)
    moves = []
    for j in range(others):
        moves.append((x_columns(x_ref, where_ref, req_count, j + 1, gate_rows), x_held.at[j]))
        for i in range(2):
            for first, size in chunks:
                span = pl.ds(i * gate_rows + first, size)
                moves.append((packed_refs[j].at[span, :], held.at[j, span, :]))
    moves.append((own_ref, own_held))
    for piece in range(piece_count):
        moves.append((down_ref.at[:, pl.ds(piece * width, width)], downs.at[piece]))
    for j in range(others):
        for piece in range(piece_count):
            span = pl.ds(2 * gate_rows + piece * down_rows, down_rows)
            moves.append((packed_refs[j].at[span, :], downs.at[(j + 1) * piece_count + piece]))
    copies = start_copies(moves, sem_ref)
    waits = iter(copies)
    _, blocks, steps, _ = x_held.shape
    gates, ups = [], []
    for j in range(others):
        next(waits).wait()
        x = x_held[j].reshape(blocks * steps, gate_rows)
        gates.append(chunked_dot(x, held.at[j, pl.ds(0, gate_rows)], chunks, waits))
        ups.append(chunked_dot(x, held.at[j, pl.ds(gate_rows, gate_rows)], chunks, waits))
    next(waits).wait()
    gate_out, up_out = own_held[0], own_held[1]
    for gate, up in zip(gates, ups):
        gate_out = gate_out + gate
        up_out = up_out + up
    activated = (jax.nn.gelu(gate_out, approximate=True) * up_out).astype(jnp.bfloat16)
    sends = []
    for index in range(req_count * piece_count):
        next(waits).wait()
        part = jnp.dot(activated, downs[index], preferred_element_type=jnp.float32)
        part = part.astype(jnp.bfloat16)
        for i in range(blocks):
            parts_ref[index, i] = part[i * steps : (i + 1) * steps]
        sends.append(
            pltpu.make_async_copy(
                parts_ref.at[index],
                out_ref.at[:, :, pl.ds(index * width, width)],
                sem_ref.at[len(copies) + index],
            )
        )
        sends[-1].start()
    for send in sends:
        send.wait()


def live_rows(
    seq_index, prompt_shape, pool_rows, group_of, prompt_lengths, tail_lengths, page_table
):
    group_count, prompt_span = prompt_shape
    rows_req = group_of.shape[0]
    member = (group_of % group_count)[:, None] == jnp.arange(group_count, dtype=jnp.int32)[None, :]
    prompt_pos = seq_index * prompt_span + jnp.arange(prompt_span, dtype=jnp.int32)
    prompt_live = prompt_pos[None, :] < prompt_lengths[:, None]
    prompt_mask = (member[:, :, None] & prompt_live[None, :, :]).reshape(
        rows_req, group_count * prompt_span
    )
    slot_count = pool_rows // PAGE
    table_row = page_table[0]
    table_len = table_row.shape[0]
    tail_pages = table_len // rows_req
    slot_ids = seq_index * slot_count + jnp.arange(slot_count, dtype=jnp.int32)
    matches = table_row[None, :] == slot_ids[:, None]
    entries = jnp.sum(
        jnp.where(matches, jnp.arange(table_len, dtype=jnp.int32)[None, :], 0), axis=1
    )
    owners = jnp.repeat(entries // tail_pages, PAGE)
    tail_pos = jnp.repeat(entries % tail_pages, PAGE) * PAGE + jnp.tile(
        jnp.arange(PAGE, dtype=jnp.int32), slot_count
    )
    tail_mask = (owners[None, :] == jnp.arange(rows_req, dtype=jnp.int32)[:, None]) & (
        tail_pos[None, :] < tail_lengths[:, None]
    )
    return jnp.concatenate([prompt_mask, tail_mask], axis=1)


def general_attention(
    seq_index,
    seq_count,
    rows_req,
    step_count,
    out_rows,
    projected,
    q_gain,
    k_gain,
    live,
    prompt_keys,
    prompt_values,
    tail_keys,
    tail_values,
):
    group_size = H // KV
    share = projected.shape[0]
    tokens = rows_req * step_count
    heads = normalize(projected.reshape(share, QKV // HD, HD))
    gains = jnp.concatenate(
        [
            jnp.broadcast_to(q_gain, (H, HD)),
            jnp.broadcast_to(k_gain, (KV, HD)),
            jnp.ones((KV, HD), jnp.float32),
        ]
    )
    mine = (heads * gains).astype(jnp.bfloat16).reshape(share, QKV)
    qkv = gather_rows(mine, seq_count)
    queries = qkv[:, : H * HD]
    keys_new = qkv[:, H * HD : (H + KV) * HD]
    values_new = qkv[:, (H + KV) * HD :]

    query_groups = queries.reshape(rows_req, step_count, KV, group_size, HD)
    mask = live[:, None, None, None, :]
    keys = jnp.concatenate([prompt_keys, tail_keys]).reshape(-1, KV, HD)
    values = jnp.concatenate([prompt_values, tail_values]).reshape(-1, KV, HD)
    scores = jnp.einsum("rskgd,pkd->rskgp", query_groups, keys, preferred_element_type=jnp.float32)
    scores = jnp.where(mask, scores, NEGATIVE)
    block_top = jnp.max(scores, axis=4)
    probs = jnp.where(mask, jnp.exp(scores - block_top[..., None]), 0.0)
    block_total = jnp.sum(probs, axis=4)
    block_accum = jnp.einsum(
        "rskgp,pkd->rskgd",
        probs.astype(jnp.bfloat16),
        values,
        preferred_element_type=jnp.float32,
    )

    stats = split_three(jnp.stack([block_top, block_total])).reshape(6, tokens, H)
    per_head = seq_count // H
    stats = jnp.repeat(stats.transpose(2, 0, 1).reshape(H, -1, out_rows), per_head, axis=0)
    accum_blocks = (
        block_accum.astype(jnp.bfloat16).reshape(tokens, seq_count, out_rows).transpose(1, 0, 2)
    )
    got = exchange(jnp.concatenate([accum_blocks, stats], axis=1), "seq")
    got_accum = got[:, :tokens].astype(jnp.float32)
    got_stats = got[:, tokens:].astype(jnp.float32).reshape(seq_count, 2 * 3, tokens)
    got_top = got_stats[:, 0] + got_stats[:, 2] + got_stats[:, 4]
    got_total = got_stats[:, 1] + got_stats[:, 3] + got_stats[:, 5]

    first_col = seq_index * out_rows
    head = first_col // HD
    kv_head = head // group_size
    head_queries = lax.dynamic_slice_in_dim(queries, head * HD, HD, 1)
    head_keys = lax.dynamic_slice_in_dim(keys_new, kv_head * HD, HD, 1)
    head_values = lax.dynamic_slice_in_dim(
        values_new, kv_head * HD + first_col % HD, out_rows, 1
    ).astype(jnp.float32)
    new_scores = jnp.dot(head_queries, head_keys.T, preferred_element_type=jnp.float32)
    token_ids = jnp.arange(tokens, dtype=jnp.int32)
    causal = (token_ids[:, None] // step_count == token_ids[None, :] // step_count) & (
        token_ids[:, None] >= token_ids[None, :]
    )
    new_scores = jnp.where(causal, new_scores, NEGATIVE)
    highest = jnp.maximum(jnp.max(got_top, axis=0), jnp.max(new_scores, axis=1))
    weights = jnp.exp(got_top - highest[None])
    new_probs = jnp.where(causal, jnp.exp(new_scores - highest[:, None]), 0.0)
    denominator = jnp.sum(got_total * weights, axis=0) + jnp.sum(new_probs, axis=1)
    numerator = jnp.sum(got_accum * weights[..., None], axis=0) + jnp.dot(
        new_probs, head_values, precision=lax.Precision.HIGHEST
    )
    return (numerator / denominator[:, None]).astype(jnp.bfloat16)


def on_device(
    req_count,
    seq_count,
    hidden_in,
    attn_gain,
    q_gain,
    k_gain,
    post_attn_gain,
    ffn_gain,
    post_ffn_gain,
    w_qkv,
    w_out,
    w_gate,
    w_up,
    w_down,
    prompt_keys,
    prompt_values,
    tail_keys,
    tail_values,
    group_of,
    prompt_lengths,
    tail_lengths,
    page_table,
):
    seq_index = lax.axis_index("seq")
    req_index = lax.axis_index("req")
    rows_req, step_count, _ = hidden_in.shape
    group_size = H // KV
    tokens = rows_req * step_count
    share = tokens // seq_count

    def shifted(values):
        return [values] + [
            lax.ppermute(values, "req", [(i, (i + j) % req_count) for i in range(req_count)])
            for j in range(1, req_count)
        ]

    where = jnp.stack([seq_index, req_index]).astype(jnp.int32)
    in_rows = w_qkv.shape[0]
    out_rows = w_out.shape[0]
    if in_rows % 128 == 0:
        normed_cols = call(
            norm_columns_kernel,
            "norm_columns",
            jax.ShapeDtypeStruct((tokens, in_rows), jnp.bfloat16),
            seq_index.astype(jnp.int32).reshape(1),
            hidden_in,
            attn_gain.reshape(1, D),
            limit=56,
        )
    else:
        normed = (normalize(hidden_in.astype(jnp.float32)) * attn_gain).astype(jnp.bfloat16)
        normed_cols = lax.dynamic_slice_in_dim(normed, seq_index * in_rows, in_rows, 2)
        normed_cols = normed_cols.reshape(tokens, in_rows)
    normed_cols, w_out_late = tie(normed_cols, w_out)
    normed_blocks = shifted(normed_cols)
    ordered = []
    for i in range(req_count):
        chosen = normed_blocks[0]
        for j in range(1, req_count):
            chosen = jnp.where((req_index - i) % req_count == j, normed_blocks[j], chosen)
        ordered.append(chosen)
    normed_all = jnp.concatenate(ordered)
    normed_all, gate_late, up_late, down_late = tie(normed_all, w_gate, w_up, w_down)
    out_blocks = shifted(w_out_late)
    width = w_gate.shape[1]
    pieces = [down_late[:, c : c + width] for c in range(0, w_down.shape[1], width)]
    packed = shifted(jnp.concatenate([gate_late, up_late] + pieces))[1:]

    qkv_part = jnp.dot(normed_all, w_qkv, preferred_element_type=jnp.float32)
    qkv_cols = w_qkv.shape[1]
    qkv_blocks = (
        (qkv_part * LINK_SCALE)
        .astype(jnp.float16)
        .reshape(req_count * seq_count, share, qkv_cols)
    )
    qkv_got = exchange(qkv_blocks, ("req", "seq"))
    qkv_got = qkv_got.reshape(req_count, seq_count, share, qkv_cols)
    projected = jnp.sum(qkv_got.astype(jnp.float32), axis=1) * (1.0 / LINK_SCALE)
    live = live_rows(
        seq_index, prompt_keys.shape[:2], tail_keys.shape[1], group_of, prompt_lengths,
        tail_lengths, page_table,
    )
    caches = [
        array.reshape(-1, KV * HD) for array in (prompt_keys, prompt_values, tail_keys, tail_values)
    ]
    direct = share == step_count and out_rows % 128 == 0 and tokens == 64 and qkv_cols % HD == 0
    if direct:
        q_blocks, new_keys, new_values = call(
            head_norm_kernel,
            "head_norm",
            (
                jax.ShapeDtypeStruct((seq_count, share, H * HD), jnp.bfloat16),
                jax.ShapeDtypeStruct((8, KV * HD), jnp.float32),
                jax.ShapeDtypeStruct((8, KV * HD), jnp.float32),
            ),
            where,
            projected,
            jnp.stack([q_gain, k_gain]),
        )
        q_got, out_blocks = tie(exchange(q_blocks, "seq"), out_blocks)
        live = jnp.repeat(live.astype(jnp.float32), step_count, axis=0)
        sent = call(
            functools.partial(block_kernel, step_count),
            "block_attention",
            jax.ShapeDtypeStruct((seq_count, tokens + 16, out_rows), jnp.bfloat16),
            where,
            q_got,
            live,
            new_keys,
            new_values,
            jnp.concatenate([caches[0], caches[2]]),
            jnp.concatenate([caches[1], caches[3]]),
        )
        got = exchange(sent, "seq")
        out_part = call(
            functools.partial(out_kernel, req_count),
            "combine_out",
            jax.ShapeDtypeStruct((seq_count, share, D), jnp.bfloat16),
            where,
            got,
            *out_blocks,
            scratch=[pltpu.VMEM((128, 128), jnp.float32)],
        )
    else:
        projected = projected.transpose(1, 0, 2).reshape(share, QKV)
        attention_cols = general_attention(
            seq_index, seq_count, rows_req, step_count, out_rows, projected, q_gain, k_gain,
            live, *caches,
        )
        out_part = jnp.concatenate(
            [jnp.dot(attention_cols, w, preferred_element_type=jnp.float32) for w in out_blocks],
            axis=1,
        )
        out_part = out_part.astype(jnp.bfloat16).reshape(seq_count, share, D)
    ffn_blocks, residual = call(
        functools.partial(residual_kernel, req_count),
        "residual_norms",
        (
            jax.ShapeDtypeStruct((seq_count, share, D), jnp.bfloat16),
            jax.ShapeDtypeStruct((share, D), jnp.float32),
        ),
        where,
        exchange(out_part, "seq"),
        hidden_in.reshape(seq_count, share, D),
        post_attn_gain.reshape(1, D),
        ffn_gain.reshape(1, D),
    )
    ffn_in = exchange(ffn_blocks, "seq")
    gate_rows = w_gate.shape[0]
    chunk_count = 2 * len(chunks_of(gate_rows))
    x_shape = (seq_count, share, gate_rows)
    own_part = call(
        functools.partial(own_kernel, req_count),
        "own_gate_up",
        jax.ShapeDtypeStruct((2, tokens, width), jnp.float32),
        where,
        ffn_in,
        w_gate,
        w_up,
        scratch=[
            pltpu.VMEM(x_shape, jnp.bfloat16),
            pltpu.VMEM((2,) + w_gate.shape, jnp.bfloat16),
            pltpu.SemaphoreType.DMA((1 + chunk_count,)),
        ],
        hbm_from=1,
        limit=56,
    )
    copy_count = (req_count - 1) * (1 + chunk_count) + 1 + D // width
    down_part = call(
        functools.partial(ffn_kernel, req_count, gate_rows),
        "feed_forward",
        jax.ShapeDtypeStruct((seq_count, share, D), jnp.bfloat16),
        where,
        ffn_in,
        own_part,
        w_down,
        *packed,
        scratch=[
            pltpu.VMEM((req_count - 1,) + x_shape, jnp.bfloat16),
            pltpu.VMEM((2, tokens, width), jnp.float32),
            pltpu.VMEM((D // width, w_down.shape[0], width), jnp.bfloat16),
            pltpu.VMEM((D // width, seq_count, share, width), jnp.bfloat16),
            pltpu.VMEM((req_count - 1, 2 * gate_rows, width), jnp.bfloat16),
            pltpu.SemaphoreType.DMA((copy_count + D // width,)),
        ],
        hbm_from=1,
        out_space=pltpu.HBM,
        limit=56,
    )
    layer_blocks = call(
        functools.partial(last_kernel, req_count),
        "last_norm",
        jax.ShapeDtypeStruct((seq_count, share, D), jnp.bfloat16),
        where,
        exchange(down_part, "seq"),
        residual,
        post_ffn_gain.reshape(1, D),
    )
    return exchange(layer_blocks, "seq").reshape(rows_req, step_count, D)


def solution(mesh):
    return jax.shard_map(
        functools.partial(on_device, mesh.shape["req"], mesh.shape["seq"]),
        mesh=mesh,
        in_specs=(
            P("req", None, None),
            P(),
            P(),
            P(),
            P(),
            P(),
            P(),
            P("seq", "req"),
            P("seq", "req"),
            P("req", "seq"),
            P("req", "seq"),
            P("seq", "req"),
            P("req", "seq", None),
            P("req", "seq", None),
            P("req", "seq", None),
            P("req", "seq", None),
            P("req"),
            P("req"),
            P("req"),
            P("req", None),
        ),
        out_specs=P("req", None, None),
        check_vma=False,
    )
```

profile of v0, /device:TPU:0, one launch (start us, length us, event | category | flops | bytes accessed | tf_op | source)
XLA Modules:
  0.0 125.0 jit_solution(13745067431050162934)
XLA Ops:
  0.0 0.0 copy-start
  0.0 1.9 %norm_columns.1 = bf16[64,128]{1,0:T(8,128)(2,1)} custom-call(s32[1]{0:T(128)} %bitcast.where_ref, bf16[16,4,2048]{2,1,0:T(4,128)(2,1)} %hidden_ref.3, f32[1,2048]{1,0:T(1,128)} %bitcast.32), custom_call_target="tpu_custom_call" | custom-call | tf_op jit(solution)/shard_map/norm_columns/pallas_call | solution.py:60
  1.9 3.0 %collective-permute-start = (bf16[64,128]{1,0:T(8,128)(2,1)}, bf16[64,128]{1,0:T(8,128)(2,1)S(1)}, u32[]{:S(2)}, u32[]{:S(2)}) collective-permute-start(bf16[64,128]{1,0:T(8,128)(2,1)} %norm_columns.1), channel_id=1, source_target_pairs={{0,1},{1,0},{2,3},{3,2},{4,5},{5,4},{6,7},{7,6},{8,9},{9,8},{10,11... | collective-permute-start | bytes 49160 | tf_op jit(solution)/shard_map/ppermute | solution.py:478
  4.9 0.0 collective-permute-start.1
  4.9 0.9 select_reduce_fusion
  5.8 0.7 and_select_fusion.2
  6.5 0.1 iota_compare_fusion.1
  6.5 0.7 pad_maximum_fusion.4.gains_ref
  7.2 0.1 pad_add_fusion.where_ref
  7.3 0.0 collective-permute-done
  7.3 0.7 broadcast_select_fusion.1
  8.1 0.0 copy-done
  8.1 0.3 fusion
  8.3 0.9 reshape.106
  9.2 6.3 %all-to-all-start = ((f16[32,4,1536]{2,1,0:T(4,128)(2,1)}), f16[32,4,1536]{2,1,0:T(4,128)(2,1)S(1)}, u32[]{:S(2)}, u32[]{:S(2)}) async-start(f16[32,4,1536]{2,1,0:T(4,128)(2,1)} %reshape.106), calls=%async_computation | async-start | bytes 786432 | tf_op jit(solution)/shard_map/all_to_all | solution.py:36
  15.5 0.0 copy-done.8
  15.5 0.1 fusion.4
  15.6 0.0 copy-done.9
  15.6 0.0 copy-start.13
  15.6 0.0 copy-start.12
  15.7 0.0 copy-start.10
  15.7 0.0 copy-start.11
  15.7 2.9 %pad_maximum_fusion = bf16[3072,512]{1,0:T(8,128)(2,1)} fusion(bf16[512,512]{1,0:T(8,128)(2,1)S(1)} %get-tuple-element.34, bf16[512,512]{1,0:T(8,128)(2,1)S(1)} %get-tuple-element.33, bf16[1024,512]{1,0:T(8,128)(2,1)} %up_ref.1, bf16[1024,512]{1,0:T(8,128)(2,1)S(1)} %copy-done.9), kind=kLoop, calls=%fused_computation | loop fusion | flops 12582912 | bytes 6291456 | tf_op jit(solution)/shard_map/concatenate | solution.py:512
  18.6 1.8 %collective-permute-start.2 = (bf16[3072,512]{1,0:T(8,128)(2,1)}, bf16[3072,512]{1,0:T(8,128)(2,1)}, u32[]{:S(2)}, u32[]{:S(2)}) collective-permute-start(bf16[3072,512]{1,0:T(8,128)(2,1)} %pad_maximum_fusion), channel_id=1, source_target_pairs={{0,1},{1,0},{2,3},{3,2},{4,5},{5,4},{6,7},{7,6},{8,9},{9,8},{10,11... | collective-permute-start | bytes 9437192 | tf_op jit(solution)/shard_map/ppermute | solution.py:478
  20.4 0.1 iota_add_fusion
  20.4 8.2 %all-to-all-done = f16[32,4,1536]{2,1,0:T(4,128)(2,1)S(1)} async-done(((f16[32,4,1536]{2,1,0:T(4,128)(2,1)}), f16[32,4,1536]{2,1,0:T(4,128)(2,1)S(1)}, u32[]{:S(2)}, u32[]{:S(2)}) %all-to-all-start) | async-done | bytes 393248 | tf_op jit(solution)/shard_map/all_to_all | solution.py:36
  28.6 0.2 convert_reduce_fusion
  28.8 1.4 %head_norm.1 = (bf16[16,4,2048]{2,1,0:T(4,128)(2,1)}, f32[8,512]{1,0:T(8,128)S(1)}, f32[8,512]{1,0:T(8,128)S(1)}) custom-call(s32[2]{0:T(128)S(1)} %pad_add_fusion.where_ref, f32[2,4,1536]{2,1,0:T(4,128)S(1)} %broadcast_multiply_fusion.projected_ref, f32[2,256]{1,0:T(2,128)S(1)} %pad_maximum_fusion.4.gains_ref), custom_call_target="tpu_custom_call" | custom-call | tf_op jit(solution)/shard_map/head_norm/pallas_call | solution.py:60
  30.2 3.5 %all-to-all-start.1 = ((bf16[16,4,2048]{2,1,0:T(4,128)(2,1)}), bf16[16,4,2048]{2,1,0:T(4,128)(2,1)S(1)}, u32[]{:S(2)}, u32[]{:S(2)}) async-start(bf16[16,4,2048]{2,1,0:T(4,128)(2,1)} %get-tuple-element.21), calls=%async_computation.1 | async-start | bytes 524288 | tf_op jit(solution)/shard_map/all_to_all | solution.py:36
  33.8 0.0 copy-done.13
  33.8 0.1 lt.59
  33.9 0.1 add.58
  33.9 0.1 broadcast_in_dim.20
  34.0 0.1 eq.68
  34.1 0.1 and.47
  34.2 0.0 copy-done.12
  34.2 0.1 fusion.1
  34.4 0.0 copy-start.1
  34.4 0.0 copy-start.5
  34.4 0.0 copy-start.6
  34.4 0.0 copy-done.10
  34.4 0.0 copy-done.11
  34.4 1.2 pad_maximum_fusion.1
  35.6 0.0 collective-permute-done.1.refs_1_
  35.6 8.2 %all-to-all-done.1.q_ref = bf16[16,4,2048]{2,1,0:T(4,128)(2,1)S(1)} async-done(((bf16[16,4,2048]{2,1,0:T(4,128)(2,1)}), bf16[16,4,2048]{2,1,0:T(4,128)(2,1)S(1)}, u32[]{:S(2)}, u32[]{:S(2)}) %all-to-all-start.1) | async-done | bytes 262176 | tf_op jit(solution)/shard_map/all_to_all | solution.py:36
  43.8 2.7 %block_attention.1 = bf16[16,80,128]{2,1,0:T(8,128)(2,1)S(1)} custom-call(s32[2]{0:T(128)S(1)} %pad_add_fusion.where_ref, bf16[16,4,2048]{2,1,0:T(4,128)(2,1)S(1)} %all-to-all-done.1.q_ref, f32[64,512]{1,0:T(8,128)S(1)} %reshape.107.live_ref, f32[8,512]{1,0:T(8,128)S(1)} %get-tuple-element.24.new_k_ref, f32[8,512]{1,0:T(8,128)S(1)} %get-tuple-element.25.new_v_ref, ...), custom_call_target="tpu_custom_call" | custom-call | tf_op jit(solution)/shard_map/block_attention/pallas_call | solution.py:60
  46.4 13.9 %all_to_all.35.got_ref = bf16[16,80,128]{2,1,0:T(8,128)(2,1)S(1)} all-to-all(bf16[16,80,128]{2,1,0:T(8,128)(2,1)S(1)} %block_attention.1), channel_id=1, replica_groups=mesh['seq'=16,'req'=2] {'seq'}, dimensions={0} | all-to-all | bytes 655360 | tf_op jit(solution)/shard_map/all_to_all | solution.py:36
  60.3 0.0 copy-done.2
  60.3 1.3 %combine_out.1 = bf16[16,4,2048]{2,1,0:T(4,128)(2,1)S(1)} custom-call(s32[2]{0:T(128)S(1)} %pad_add_fusion.where_ref, bf16[16,80,128]{2,1,0:T(8,128)(2,1)S(1)} %all_to_all.35.got_ref, bf16[128,1024]{1,0:T(8,128)(2,1)S(1)} %copy-done.2, bf16[128,1024]{1,0:T(8,128)(2,1)S(1)} %collective-permute-done.1.refs_1_), custom_call_target="tpu_custom_call" | custom-call | tf_op jit(solution)/shard_map/combine_out/pallas_call | solution.py:60
  61.6 13.1 %all_to_all.36.got_ref = bf16[16,4,2048]{2,1,0:T(4,128)(2,1)S(1)} all-to-all(bf16[16,4,2048]{2,1,0:T(4,128)(2,1)S(1)} %combine_out.1), channel_id=1, replica_groups=mesh['seq'=16,'req'=2] {'seq'}, dimensions={0} | all-to-all | bytes 524288 | tf_op jit(solution)/shard_map/all_to_all | solution.py:36
  74.7 0.0 copy-done.3
  74.7 0.0 copy-done.1
  74.7 0.0 copy-done.5
  74.7 0.0 copy-done.6
  74.7 0.9 residual_norms.1
  75.6 13.3 %all_to_all.37.x_ref = bf16[16,4,2048]{2,1,0:T(4,128)(2,1)} all-to-all(bf16[16,4,2048]{2,1,0:T(4,128)(2,1)S(1)} %get-tuple-element.28), channel_id=1, replica_groups=mesh['seq'=16,'req'=2] {'seq'}, dimensions={0} | all-to-all | bytes 524288 | tf_op jit(solution)/shard_map/all_to_all | solution.py:36
  88.9 3.2 %own_gate_up.1.own_ref = f32[2,64,512]{2,1,0:T(8,128)} custom-call(s32[2]{0:T(128)} %copy-done.3, bf16[16,4,2048]{2,1,0:T(4,128)(2,1)} %all_to_all.37.x_ref, bf16[1024,512]{1,0:T(8,128)(2,1)} %gate_ref.1, bf16[1024,512]{1,0:T(8,128)(2,1)} %up_ref.1), custom_call_target="tpu_custom_call" | custom-call | tf_op jit(solution)/shard_map/own_gate_up/pallas_call | solution.py:60
  92.2 0.0 copy-start.7
  92.2 0.0 collective-permute-done.2.refs_0_
  92.2 4.2 %feed_forward.1 = bf16[16,4,2048]{2,1,0:T(4,128)(2,1)} custom-call(s32[2]{0:T(128)} %copy-done.3, bf16[16,4,2048]{2,1,0:T(4,128)(2,1)} %all_to_all.37.x_ref, f32[2,64,512]{2,1,0:T(8,128)} %own_gate_up.1.own_ref, bf16[512,1024]{1,0:T(8,128)(2,1)} %down_ref.1, bf16[3072,512]{1,0:T(8,128)(2,1)} %collective-permute-done.2.refs_0_), custom_call_target="tpu_custom_call" | custom-call | tf_op jit(solution)/shard_map/feed_forward/pallas_call | solution.py:60
  96.4 14.2 %all_to_all.38.got_ref = bf16[16,4,2048]{2,1,0:T(4,128)(2,1)S(1)} all-to-all(bf16[16,4,2048]{2,1,0:T(4,128)(2,1)} %feed_forward.1), channel_id=1, replica_groups=mesh['seq'=16,'req'=2] {'seq'}, dimensions={0} | all-to-all | bytes 524288 | tf_op jit(solution)/shard_map/all_to_all | solution.py:36
  110.7 0.8 last_norm.1
  111.4 12.8 %all_to_all.39 = bf16[16,4,2048]{2,1,0:T(4,128)(2,1)S(1)} all-to-all(bf16[16,4,2048]{2,1,0:T(4,128)(2,1)S(1)} %last_norm.1), channel_id=1, replica_groups=mesh['seq'=16,'req'=2] {'seq'}, dimensions={0} | all-to-all | bytes 524288 | tf_op jit(solution)/shard_map/all_to_all | solution.py:36
  124.3 0.7 copy.24
  (16 shorter events, 0.1 us)
Async XLA Ops:
  0.0 8.1 %copy-start = (bf16[128,1536]{1,0:T(8,128)(2,1)S(1)}, bf16[128,1536]{1,0:T(8,128)(2,1)}, u32[]{:S(2)}) copy-start(bf16[128,1536]{1,0:T(8,128)(2,1)} %param.27) | copy-start | bytes 1179652
  0.0 15.6 %copy-start.9 = (bf16[1024,512]{1,0:T(8,128)(2,1)S(1)}, bf16[1024,512]{1,0:T(8,128)(2,1)}, u32[]{:S(2)}) copy-start(bf16[1024,512]{1,0:T(8,128)(2,1)} %gate_ref.1) | copy-start | bytes 3145732
  0.0 15.5 %copy-start.8 = (bf16[512,1024]{1,0:T(8,128)(2,1)S(1)}, bf16[512,1024]{1,0:T(8,128)(2,1)}, u32[]{:S(2)}) copy-start(bf16[512,1024]{1,0:T(8,128)(2,1)} %down_ref.1) | copy-start | bytes 3145732
  1.9 5.4 %collective-permute-start = (bf16[64,128]{1,0:T(8,128)(2,1)}, bf16[64,128]{1,0:T(8,128)(2,1)S(1)}, u32[]{:S(2)}, u32[]{:S(2)}) collective-permute-start(bf16[64,128]{1,0:T(8,128)(2,1)} %norm_columns.1), channel_id=1, source_target_pairs={{0,1},{1,0},{2,3},{3,2},{4,5},{5,4},{6,7},{7,6},{8,9},{9,8},{10,11... | collective-permute-start | bytes 49160 | tf_op jit(solution)/shard_map/ppermute | solution.py:478
  4.9 30.7 %collective-permute-start.1 = (bf16[128,1024]{1,0:T(8,128)(2,1)}, bf16[128,1024]{1,0:T(8,128)(2,1)S(1)}, u32[]{:S(2)}, u32[]{:S(2)}) collective-permute-start(bf16[128,1024]{1,0:T(8,128)(2,1)} %refs_0_), channel_id=1, source_target_pairs={{0,1},{1,0},{2,3},{3,2},{4,5},{5,4},{6,7},{7,6},{8,9},{9,8},{10,11... | collective-permute-start | bytes 786440 | tf_op jit(solution)/shard_map/ppermute | solution.py:478
  7.3 67.4 %copy-start.3 = (s32[2]{0:T(128)}, s32[2]{0:T(128)S(1)}, u32[]{:S(2)}) copy-start(s32[2]{0:T(128)S(1)} %pad_add_fusion.where_ref) | copy-start | bytes 28
  9.2 19.5 %all-to-all-start = ((f16[32,4,1536]{2,1,0:T(4,128)(2,1)}), f16[32,4,1536]{2,1,0:T(4,128)(2,1)S(1)}, u32[]{:S(2)}, u32[]{:S(2)}) async-start(f16[32,4,1536]{2,1,0:T(4,128)(2,1)} %reshape.106), calls=%async_computation | async-start | bytes 786432 | tf_op jit(solution)/shard_map/all_to_all | solution.py:36
  15.6 18.1 %copy-start.13 = (s32[2]{0:T(128)S(1)}, s32[2]{0:T(128)}, u32[]{:S(2)}) copy-start(s32[2]{0:T(128)} %param.37) | copy-start | bytes 28
  15.6 18.5 %copy-start.12 = (s32[16]{0:T(128)S(1)}, s32[16]{0:T(128)}, u32[]{:S(2)}) copy-start(s32[16]{0:T(128)} %param.38) | copy-start | bytes 196
  15.7 18.8 %copy-start.10 = (bf16[1,256,512]{2,1,0:T(8,128)(2,1)S(1)}, bf16[1,256,512]{2,1,0:T(8,128)(2,1)}, u32[]{:S(2)}) copy-start(bf16[1,256,512]{2,1,0:T(8,128)(2,1)} %param.34) | copy-start | bytes 786436
  15.7 18.7 %copy-start.11 = (bf16[2,128,512]{2,1,0:T(8,128)(2,1)S(1)}, bf16[2,128,512]{2,1,0:T(8,128)(2,1)}, u32[]{:S(2)}) copy-start(bf16[2,128,512]{2,1,0:T(8,128)(2,1)} %param.32) | copy-start | bytes 786436
  18.6 41.7 %copy-start.2 = (bf16[128,1024]{1,0:T(8,128)(2,1)S(1)}, bf16[128,1024]{1,0:T(8,128)(2,1)}, u32[]{:S(2)}) copy-start(bf16[128,1024]{1,0:T(8,128)(2,1)} %refs_0_) | copy-start | bytes 786436
  18.6 73.6 %collective-permute-start.2 = (bf16[3072,512]{1,0:T(8,128)(2,1)}, bf16[3072,512]{1,0:T(8,128)(2,1)}, u32[]{:S(2)}, u32[]{:S(2)}) collective-permute-start(bf16[3072,512]{1,0:T(8,128)(2,1)} %pad_maximum_fusion), channel_id=1, source_target_pairs={{0,1},{1,0},{2,3},{3,2},{4,5},{5,4},{6,7},{7,6},{8,9},{9,8},{10,11... | collective-permute-start | bytes 9437192 | tf_op jit(solution)/shard_map/ppermute | solution.py:478
  30.2 13.5 %all-to-all-start.1 = ((bf16[16,4,2048]{2,1,0:T(4,128)(2,1)}), bf16[16,4,2048]{2,1,0:T(4,128)(2,1)S(1)}, u32[]{:S(2)}, u32[]{:S(2)}) async-start(bf16[16,4,2048]{2,1,0:T(4,128)(2,1)} %get-tuple-element.21), calls=%async_computation.1 | async-start | bytes 524288 | tf_op jit(solution)/shard_map/all_to_all | solution.py:36
  34.4 40.3 %copy-start.1 = (bf16[16,4,2048]{2,1,0:T(4,128)(2,1)S(1)}, bf16[16,4,2048]{2,1,0:T(4,128)(2,1)}, u32[]{:S(2)}) copy-start(bf16[16,4,2048]{2,1,0:T(4,128)(2,1)} %hidden_ref.3) | copy-start | bytes 786436
  34.4 40.3 %copy-start.5 = (f32[2048]{0:T(1024)S(1)}, f32[2048]{0:T(1024)}, u32[]{:S(2)}) copy-start(f32[2048]{0:T(1024)} %param.24) | copy-start | bytes 24580
  34.4 40.3 %copy-start.6 = (f32[2048]{0:T(1024)S(1)}, f32[2048]{0:T(1024)}, u32[]{:S(2)}) copy-start(f32[2048]{0:T(1024)} %param.25) | copy-start | bytes 24580
  92.2 18.5 %copy-start.4 = (s32[2]{0:T(128)S(1)}, s32[2]{0:T(128)}, u32[]{:S(2)}) copy-start(s32[2]{0:T(128)} %copy-done.3) | copy-start | bytes 28
  92.2 18.5 %copy-start.7 = (f32[2048]{0:T(1024)S(1)}, f32[2048]{0:T(1024)}, u32[]{:S(2)}) copy-start(f32[2048]{0:T(1024)} %param.26) | copy-start | bytes 24580
where the time goes:
time: 126 us; the launch traced here: 125 us
  blocking collectives  67.3 us (53%)
  Pallas kernels  16.4 us (13%)
  waiting for transfers between devices  16.4 us (13%)
  starting transfers between devices  14.6 us (12%)
  other arithmetic  7.55 us (6%)
  local copies, waits for them, and re-layouts  2.18 us (2%)
    all_to_all x5, blocking collectives, exchange(): lax.all_to_all(blocks, axes, split_axis=0, concat_axis=0, tiled=True, axi...  67.3 us
    all_to_all x2, waiting for transfers between devices, exchange(): lax.all_to_all(blocks, axes, split_axis=0, concat_axis=0, tiled=True, axi...  16.4 us
    pallas_call x8, Pallas kernels, call(): pl.pallas_call(kernel, name=name, out_shape=out_shape, in_specs=in_specs,...  16.4 us
    all_to_all x2, starting transfers between devices, exchange(): lax.all_to_all(blocks, axes, split_axis=0, concat_axis=0, tiled=True, axi...  9.88 us
    ppermute x3, starting transfers between devices, shifted(): lax.ppermute(values, 'req', [(i, (i + j) % req_count) for i in range(req_...  4.75 us
    concatenate x1, other arithmetic, on_device(): packed = shifted(jnp.concatenate([gate_late, up_late] + pieces))[1:]  2.89 us
  transfers between devices with their start and end apart: 5, of which 2 were waited for; matrix products, arithmetic and copies ran while one was open for 7% of the time, Pallas kernels for 8%

commit v1 on v0

--- a/solution.py
+++ b/solution.py
@@ -62,7 +62,11 @@
         name=name,
         out_shape=out_shape,
         in_specs=in_specs,
-        out_specs=jax.tree.map(lambda _: pl.BlockSpec(memory_space=out_space), out_shape),
+        out_specs=(
+            tuple(pl.BlockSpec(memory_space=space) for space in out_space)
+            if isinstance(out_space, tuple)
+            else jax.tree.map(lambda _: pl.BlockSpec(memory_space=out_space), out_shape)
+        ),
         scratch_shapes=scratch,
         compiler_params=pltpu.CompilerParams(vmem_limit_bytes=limit * 1024 * 1024),
     )(*operands)
@@ -77,7 +81,7 @@
     out_ref[...] = normed.reshape(out_ref.shape).astype(jnp.bfloat16)
 
 
-def head_norm_kernel(where_ref, projected_ref, gains_ref, q_ref, k_ref, v_ref):
+def head_norm_kernel(where_ref, projected_ref, gains_ref, q_ref, k_ref, v_ref, held_ref, sem_ref):
     width = projected_ref.shape[2]
     copies, rows, _ = q_ref.shape
     fill = jnp.zeros((k_ref.shape[0] - rows, HD), jnp.float32)
@@ -86,14 +90,22 @@
         values = normalize(projected_ref[half, :, first : first + HD])
         if head < H:
             values = (values * gains_ref[0:1, :]).astype(jnp.bfloat16)
-            for i in range(copies):
-                q_ref[i, :, head * HD : (head + 1) * HD] = values
+            held_ref[:, head * HD : (head + 1) * HD] = values
+            if head == H - 1:
+                sends = [
+                    pltpu.make_async_copy(held_ref, q_ref.at[i], sem_ref.at[i])
+                    for i in range(copies)
+                ]
+                for send in sends:
+                    send.start()
         else:
             if head < H + KV:
                 values = values * gains_ref[1:2, :]
             values = values.astype(jnp.bfloat16).astype(jnp.float32)
             target, slot = (k_ref, head - H) if head < H + KV else (v_ref, head - H - KV)
             target[:, slot * HD : (slot + 1) * HD] = jnp.concatenate([values, fill])
+    for send in sends:
+        send.wait()
 
 
 def dot_last(a, b):
@@ -257,7 +269,7 @@
     return total
 
 
-def own_kernel(req_count, where_ref, x_ref, gate_ref, up_ref, out_ref, x_held, held, sem_ref):
+def own_kernel(req_count, where_ref, x_ref, gate_ref, up_ref, out_ref, x_held, held, parts_ref, sem_ref):
     rows = gate_ref.shape[0]
     chunks = chunks_of(rows)
     moves = [(x_columns(x_ref, where_ref, req_count, 0, rows), x_held)]
@@ -269,8 +281,15 @@
     blocks, steps, _ = x_held.shape
     next(waits).wait()
     x = x_held[...].reshape(blocks * steps, rows)
+    sends = []
     for i in range(2):
-        out_ref[i] = chunked_dot(x, held.at[i], chunks, waits)
+        parts_ref[i] = chunked_dot(x, held.at[i], chunks, waits)
+        sends.append(
+            pltpu.make_async_copy(parts_ref.at[i], out_ref.at[i], sem_ref.at[len(moves) + i])
+        )
+        sends[-1].start()
+    for send in sends:
+        send.wait()
 
 
 def ffn_kernel(req_count, gate_rows, where_ref, x_ref, own_ref, down_ref, *refs):
@@ -541,6 +560,11 @@
             where,
             projected,
             jnp.stack([q_gain, k_gain]),
+            scratch=[
+                pltpu.VMEM((share, H * HD), jnp.bfloat16),
+                pltpu.SemaphoreType.DMA((seq_count,)),
+            ],
+            out_space=(pltpu.HBM, pltpu.VMEM, pltpu.VMEM),
         )
         q_got, out_blocks = tie(exchange(q_blocks, "seq"), out_blocks)
         live = jnp.repeat(live.astype(jnp.float32), step_count, axis=0)
@@ -605,9 +629,11 @@
         scratch=[
             pltpu.VMEM(x_shape, jnp.bfloat16),
             pltpu.VMEM((2,) + w_gate.shape, jnp.bfloat16),
-            pltpu.SemaphoreType.DMA((1 + chunk_count,)),
+            pltpu.VMEM((2, tokens, width), jnp.float32),
+            pltpu.SemaphoreType.DMA((3 + chunk_count,)),
         ],
         hbm_from=1,
+        out_space=pltpu.HBM,
         limit=56,
     )
     copy_count = (req_count - 1) * (1 + chunk_count) + 1 + D // width

time: 126 us -> 126 us (level)
  no operation moved by 1% of the time
where the time goes in v1:
time: 126 us; the launch traced here: 125 us
  blocking collectives  67.3 us (53%)
  Pallas kernels  16.4 us (13%)
  waiting for transfers between devices  16.4 us (13%)
  starting transfers between devices  14.6 us (12%)
  other arithmetic  7.55 us (6%)
  local copies, waits for them, and re-layouts  2.18 us (2%)
    all_to_all x5, blocking collectives, exchange(): lax.all_to_all(blocks, axes, split_axis=0, concat_axis=0, tiled=True, axi...  67.3 us
    pallas_call x8, Pallas kernels, call(): pl.pallas_call(kernel, name=name, out_shape=out_shape, in_specs=in_specs,...  16.4 us
    all_to_all x2, waiting for transfers between devices, exchange(): lax.all_to_all(blocks, axes, split_axis=0, concat_axis=0, tiled=True, axi...  16.4 us
    all_to_all x2, starting transfers between devices, exchange(): lax.all_to_all(blocks, axes, split_axis=0, concat_axis=0, tiled=True, axi...  9.89 us
    ppermute x3, starting transfers between devices, shifted(): lax.ppermute(values, 'req', [(i, (i + j) % req_count) for i in range(req_...  4.75 us
    concatenate x1, other arithmetic, on_device(): packed = shifted(jnp.concatenate([gate_late, up_late] + pieces))[1:]  2.89 us
  transfers between devices with their start and end apart: 5, of which 2 were waited for; matrix products, arithmetic and copies ran while one was open for 7% of the time, Pallas kernels for 8%

profile of v1, /device:TPU:0, one launch (start us, length us, event | category | flops | bytes accessed | tf_op | source)
XLA Modules:
  0.0 125.0 jit_solution(10058527673208826312)
XLA Ops:
  0.0 0.0 copy-start
  0.0 1.9 %norm_columns.1 = bf16[64,128]{1,0:T(8,128)(2,1)} custom-call(s32[1]{0:T(128)} %bitcast.where_ref, bf16[16,4,2048]{2,1,0:T(4,128)(2,1)} %hidden_ref.3, f32[1,2048]{1,0:T(1,128)} %bitcast.32), custom_call_target="tpu_custom_call" | custom-call | tf_op jit(solution)/shard_map/norm_columns/pallas_call | solution.py:60
  1.9 3.0 %collective-permute-start = (bf16[64,128]{1,0:T(8,128)(2,1)}, bf16[64,128]{1,0:T(8,128)(2,1)S(1)}, u32[]{:S(2)}, u32[]{:S(2)}) collective-permute-start(bf16[64,128]{1,0:T(8,128)(2,1)} %norm_columns.1), channel_id=1, source_target_pairs={{0,1},{1,0},{2,3},{3,2},{4,5},{5,4},{6,7},{7,6},{8,9},{9,8},{10,11... | collective-permute-start | bytes 49160 | tf_op jit(solution)/shard_map/ppermute | solution.py:497
  4.9 0.0 collective-permute-start.1
  4.9 0.9 select_reduce_fusion
  5.8 0.7 and_select_fusion.2
  6.5 0.1 iota_compare_fusion.1
  6.5 0.7 pad_maximum_fusion.4.gains_ref
  7.2 0.1 pad_add_fusion.where_ref
  7.3 0.0 collective-permute-done
  7.3 0.7 broadcast_select_fusion.1
  8.1 0.0 copy-done
  8.1 0.3 fusion
  8.3 0.9 reshape.106
  9.2 6.3 %all-to-all-start = ((f16[32,4,1536]{2,1,0:T(4,128)(2,1)}), f16[32,4,1536]{2,1,0:T(4,128)(2,1)S(1)}, u32[]{:S(2)}, u32[]{:S(2)}) async-start(f16[32,4,1536]{2,1,0:T(4,128)(2,1)} %reshape.106), calls=%async_computation | async-start | bytes 786432 | tf_op jit(solution)/shard_map/all_to_all | solution.py:36
  15.5 0.0 copy-done.8
  15.5 0.1 fusion.4
  15.6 0.0 copy-done.9
  15.6 0.0 copy-start.13
  15.6 0.0 copy-start.12
  15.7 0.0 copy-start.10
  15.7 0.0 copy-start.11
  15.7 2.9 %pad_maximum_fusion = bf16[3072,512]{1,0:T(8,128)(2,1)} fusion(bf16[512,512]{1,0:T(8,128)(2,1)S(1)} %get-tuple-element.34, bf16[512,512]{1,0:T(8,128)(2,1)S(1)} %get-tuple-element.33, bf16[1024,512]{1,0:T(8,128)(2,1)} %up_ref.1, bf16[1024,512]{1,0:T(8,128)(2,1)S(1)} %copy-done.9), kind=kLoop, calls=%fused_computation | loop fusion | flops 12582912 | bytes 6291456 | tf_op jit(solution)/shard_map/concatenate | solution.py:531
  18.6 1.8 %collective-permute-start.2 = (bf16[3072,512]{1,0:T(8,128)(2,1)}, bf16[3072,512]{1,0:T(8,128)(2,1)}, u32[]{:S(2)}, u32[]{:S(2)}) collective-permute-start(bf16[3072,512]{1,0:T(8,128)(2,1)} %pad_maximum_fusion), channel_id=1, source_target_pairs={{0,1},{1,0},{2,3},{3,2},{4,5},{5,4},{6,7},{7,6},{8,9},{9,8},{10,11... | collective-permute-start | bytes 9437192 | tf_op jit(solution)/shard_map/ppermute | solution.py:497
  20.4 0.1 iota_add_fusion
  20.4 8.2 %all-to-all-done = f16[32,4,1536]{2,1,0:T(4,128)(2,1)S(1)} async-done(((f16[32,4,1536]{2,1,0:T(4,128)(2,1)}), f16[32,4,1536]{2,1,0:T(4,128)(2,1)S(1)}, u32[]{:S(2)}, u32[]{:S(2)}) %all-to-all-start) | async-done | bytes 393248 | tf_op jit(solution)/shard_map/all_to_all | solution.py:36
  28.6 0.2 convert_reduce_fusion
  28.8 1.5 %head_norm.1 = (bf16[16,4,2048]{2,1,0:T(4,128)(2,1)}, f32[8,512]{1,0:T(8,128)S(1)}, f32[8,512]{1,0:T(8,128)S(1)}) custom-call(s32[2]{0:T(128)S(1)} %pad_add_fusion.where_ref, f32[2,4,1536]{2,1,0:T(4,128)S(1)} %broadcast_multiply_fusion.projected_ref, f32[2,256]{1,0:T(2,128)S(1)} %pad_maximum_fusion.4.gains_ref), custom_call_target="tpu_custom_call" | custom-call | tf_op jit(solution)/shard_map/head_norm/pallas_call | solution.py:60
  30.3 3.5 %all-to-all-start.1 = ((bf16[16,4,2048]{2,1,0:T(4,128)(2,1)}), bf16[16,4,2048]{2,1,0:T(4,128)(2,1)S(1)}, u32[]{:S(2)}, u32[]{:S(2)}) async-start(bf16[16,4,2048]{2,1,0:T(4,128)(2,1)} %get-tuple-element.21), calls=%async_computation.1 | async-start | bytes 524288 | tf_op jit(solution)/shard_map/all_to_all | solution.py:36
  33.9 0.0 copy-done.13
  33.9 0.1 lt.59
  33.9 0.1 add.58
  34.0 0.1 broadcast_in_dim.20
  34.1 0.1 eq.68
  34.2 0.1 and.47
  34.3 0.0 copy-done.12
  34.3 0.1 fusion.1
  34.5 0.0 copy-start.1
  34.5 0.0 copy-start.5
  34.5 0.0 copy-start.6
  34.5 0.0 copy-done.10
  34.5 0.0 copy-done.11
  34.5 1.2 pad_maximum_fusion.1
  35.7 0.0 collective-permute-done.1.refs_1_
  35.7 8.2 %all-to-all-done.1.q_ref = bf16[16,4,2048]{2,1,0:T(4,128)(2,1)S(1)} async-done(((bf16[16,4,2048]{2,1,0:T(4,128)(2,1)}), bf16[16,4,2048]{2,1,0:T(4,128)(2,1)S(1)}, u32[]{:S(2)}, u32[]{:S(2)}) %all-to-all-start.1) | async-done | bytes 262176 | tf_op jit(solution)/shard_map/all_to_all | solution.py:36
  43.9 2.6 %block_attention.1 = bf16[16,80,128]{2,1,0:T(8,128)(2,1)S(1)} custom-call(s32[2]{0:T(128)S(1)} %pad_add_fusion.where_ref, bf16[16,4,2048]{2,1,0:T(4,128)(2,1)S(1)} %all-to-all-done.1.q_ref, f32[64,512]{1,0:T(8,128)S(1)} %reshape.107.live_ref, f32[8,512]{1,0:T(8,128)S(1)} %get-tuple-element.24.new_k_ref, f32[8,512]{1,0:T(8,128)S(1)} %get-tuple-element.25.new_v_ref, ...), custom_call_target="tpu_custom_call" | custom-call | tf_op jit(solution)/shard_map/block_attention/pallas_call | solution.py:60
  46.5 13.9 %all_to_all.35.got_ref = bf16[16,80,128]{2,1,0:T(8,128)(2,1)S(1)} all-to-all(bf16[16,80,128]{2,1,0:T(8,128)(2,1)S(1)} %block_attention.1), channel_id=1, replica_groups=mesh['seq'=16,'req'=2] {'seq'}, dimensions={0} | all-to-all | bytes 655360 | tf_op jit(solution)/shard_map/all_to_all | solution.py:36
  60.4 0.0 copy-done.2
  60.4 1.3 %combine_out.1 = bf16[16,4,2048]{2,1,0:T(4,128)(2,1)S(1)} custom-call(s32[2]{0:T(128)S(1)} %pad_add_fusion.where_ref, bf16[16,80,128]{2,1,0:T(8,128)(2,1)S(1)} %all_to_all.35.got_ref, bf16[128,1024]{1,0:T(8,128)(2,1)S(1)} %copy-done.2, bf16[128,1024]{1,0:T(8,128)(2,1)S(1)} %collective-permute-done.1.refs_1_), custom_call_target="tpu_custom_call" | custom-call | tf_op jit(solution)/shard_map/combine_out/pallas_call | solution.py:60
  61.7 13.1 %all_to_all.36.got_ref = bf16[16,4,2048]{2,1,0:T(4,128)(2,1)S(1)} all-to-all(bf16[16,4,2048]{2,1,0:T(4,128)(2,1)S(1)} %combine_out.1), channel_id=1, replica_groups=mesh['seq'=16,'req'=2] {'seq'}, dimensions={0} | all-to-all | bytes 524288 | tf_op jit(solution)/shard_map/all_to_all | solution.py:36
  74.8 0.0 copy-done.3
  74.8 0.0 copy-done.1
  74.8 0.0 copy-done.5
  74.8 0.0 copy-done.6
  74.8 0.9 residual_norms.1
  75.7 13.3 %all_to_all.37.x_ref = bf16[16,4,2048]{2,1,0:T(4,128)(2,1)} all-to-all(bf16[16,4,2048]{2,1,0:T(4,128)(2,1)S(1)} %get-tuple-element.28), channel_id=1, replica_groups=mesh['seq'=16,'req'=2] {'seq'}, dimensions={0} | all-to-all | bytes 524288 | tf_op jit(solution)/shard_map/all_to_all | solution.py:36
  89.0 3.2 %own_gate_up.1.own_ref = f32[2,64,512]{2,1,0:T(8,128)} custom-call(s32[2]{0:T(128)} %copy-done.3, bf16[16,4,2048]{2,1,0:T(4,128)(2,1)} %all_to_all.37.x_ref, bf16[1024,512]{1,0:T(8,128)(2,1)} %gate_ref.1, bf16[1024,512]{1,0:T(8,128)(2,1)} %up_ref.1), custom_call_target="tpu_custom_call" | custom-call | tf_op jit(solution)/shard_map/own_gate_up/pallas_call | solution.py:60
  92.2 0.0 copy-start.7
  92.3 0.0 collective-permute-done.2.refs_0_
  92.3 4.2 %feed_forward.1 = bf16[16,4,2048]{2,1,0:T(4,128)(2,1)} custom-call(s32[2]{0:T(128)} %copy-done.3, bf16[16,4,2048]{2,1,0:T(4,128)(2,1)} %all_to_all.37.x_ref, f32[2,64,512]{2,1,0:T(8,128)} %own_gate_up.1.own_ref, bf16[512,1024]{1,0:T(8,128)(2,1)} %down_ref.1, bf16[3072,512]{1,0:T(8,128)(2,1)} %collective-permute-done.2.refs_0_), custom_call_target="tpu_custom_call" | custom-call | tf_op jit(solution)/shard_map/feed_forward/pallas_call | solution.py:60
  96.5 14.2 %all_to_all.38.got_ref = bf16[16,4,2048]{2,1,0:T(4,128)(2,1)S(1)} all-to-all(bf16[16,4,2048]{2,1,0:T(4,128)(2,1)} %feed_forward.1), channel_id=1, replica_groups=mesh['seq'=16,'req'=2] {'seq'}, dimensions={0} | all-to-all | bytes 524288 | tf_op jit(solution)/shard_map/all_to_all | solution.py:36
  110.7 0.8 last_norm.1
  111.4 12.8 %all_to_all.39 = bf16[16,4,2048]{2,1,0:T(4,128)(2,1)S(1)} all-to-all(bf16[16,4,2048]{2,1,0:T(4,128)(2,1)S(1)} %last_norm.1), channel_id=1, replica_groups=mesh['seq'=16,'req'=2] {'seq'}, dimensions={0} | all-to-all | bytes 524288 | tf_op jit(solution)/shard_map/all_to_all | solution.py:36
  124.3 0.7 copy.24
  (16 shorter events, 0.1 us)
Async XLA Ops:
  0.0 8.1 %copy-start = (bf16[128,1536]{1,0:T(8,128)(2,1)S(1)}, bf16[128,1536]{1,0:T(8,128)(2,1)}, u32[]{:S(2)}) copy-start(bf16[128,1536]{1,0:T(8,128)(2,1)} %param.27) | copy-start | bytes 1179652
  0.0 15.6 %copy-start.9 = (bf16[1024,512]{1,0:T(8,128)(2,1)S(1)}, bf16[1024,512]{1,0:T(8,128)(2,1)}, u32[]{:S(2)}) copy-start(bf16[1024,512]{1,0:T(8,128)(2,1)} %gate_ref.1) | copy-start | bytes 3145732
  0.0 15.5 %copy-start.8 = (bf16[512,1024]{1,0:T(8,128)(2,1)S(1)}, bf16[512,1024]{1,0:T(8,128)(2,1)}, u32[]{:S(2)}) copy-start(bf16[512,1024]{1,0:T(8,128)(2,1)} %down_ref.1) | copy-start | bytes 3145732
  1.9 5.4 %collective-permute-start = (bf16[64,128]{1,0:T(8,128)(2,1)}, bf16[64,128]{1,0:T(8,128)(2,1)S(1)}, u32[]{:S(2)}, u32[]{:S(2)}) collective-permute-start(bf16[64,128]{1,0:T(8,128)(2,1)} %norm_columns.1), channel_id=1, source_target_pairs={{0,1},{1,0},{2,3},{3,2},{4,5},{5,4},{6,7},{7,6},{8,9},{9,8},{10,11... | collective-permute-start | bytes 49160 | tf_op jit(solution)/shard_map/ppermute | solution.py:497
  4.9 30.8 %collective-permute-start.1 = (bf16[128,1024]{1,0:T(8,128)(2,1)}, bf16[128,1024]{1,0:T(8,128)(2,1)S(1)}, u32[]{:S(2)}, u32[]{:S(2)}) collective-permute-start(bf16[128,1024]{1,0:T(8,128)(2,1)} %refs_0_), channel_id=1, source_target_pairs={{0,1},{1,0},{2,3},{3,2},{4,5},{5,4},{6,7},{7,6},{8,9},{9,8},{10,11... | collective-permute-start | bytes 786440 | tf_op jit(solution)/shard_map/ppermute | solution.py:497
  7.3 67.5 %copy-start.3 = (s32[2]{0:T(128)}, s32[2]{0:T(128)S(1)}, u32[]{:S(2)}) copy-start(s32[2]{0:T(128)S(1)} %pad_add_fusion.where_ref) | copy-start | bytes 28
  9.2 19.5 %all-to-all-start = ((f16[32,4,1536]{2,1,0:T(4,128)(2,1)}), f16[32,4,1536]{2,1,0:T(4,128)(2,1)S(1)}, u32[]{:S(2)}, u32[]{:S(2)}) async-start(f16[32,4,1536]{2,1,0:T(4,128)(2,1)} %reshape.106), calls=%async_computation | async-start | bytes 786432 | tf_op jit(solution)/shard_map/all_to_all | solution.py:36
  15.6 18.2 %copy-start.13 = (s32[2]{0:T(128)S(1)}, s32[2]{0:T(128)}, u32[]{:S(2)}) copy-start(s32[2]{0:T(128)} %param.37) | copy-start | bytes 28
  15.6 18.6 %copy-start.12 = (s32[16]{0:T(128)S(1)}, s32[16]{0:T(128)}, u32[]{:S(2)}) copy-start(s32[16]{0:T(128)} %param.38) | copy-start | bytes 196
  15.7 18.8 %copy-start.10 = (bf16[1,256,512]{2,1,0:T(8,128)(2,1)S(1)}, bf16[1,256,512]{2,1,0:T(8,128)(2,1)}, u32[]{:S(2)}) copy-start(bf16[1,256,512]{2,1,0:T(8,128)(2,1)} %param.34) | copy-start | bytes 786436
  15.7 18.8 %copy-start.11 = (bf16[2,128,512]{2,1,0:T(8,128)(2,1)S(1)}, bf16[2,128,512]{2,1,0:T(8,128)(2,1)}, u32[]{:S(2)}) copy-start(bf16[2,128,512]{2,1,0:T(8,128)(2,1)} %param.32) | copy-start | bytes 786436
  18.6 41.8 %copy-start.2 = (bf16[128,1024]{1,0:T(8,128)(2,1)S(1)}, bf16[128,1024]{1,0:T(8,128)(2,1)}, u32[]{:S(2)}) copy-start(bf16[128,1024]{1,0:T(8,128)(2,1)} %refs_0_) | copy-start | bytes 786436
  18.6 73.7 %collective-permute-start.2 = (bf16[3072,512]{1,0:T(8,128)(2,1)}, bf16[3072,512]{1,0:T(8,128)(2,1)}, u32[]{:S(2)}, u32[]{:S(2)}) collective-permute-start(bf16[3072,512]{1,0:T(8,128)(2,1)} %pad_maximum_fusion), channel_id=1, source_target_pairs={{0,1},{1,0},{2,3},{3,2},{4,5},{5,4},{6,7},{7,6},{8,9},{9,8},{10,11... | collective-permute-start | bytes 9437192 | tf_op jit(solution)/shard_map/ppermute | solution.py:497
  30.3 13.6 %all-to-all-start.1 = ((bf16[16,4,2048]{2,1,0:T(4,128)(2,1)}), bf16[16,4,2048]{2,1,0:T(4,128)(2,1)S(1)}, u32[]{:S(2)}, u32[]{:S(2)}) async-start(bf16[16,4,2048]{2,1,0:T(4,128)(2,1)} %get-tuple-element.21), calls=%async_computation.1 | async-start | bytes 524288 | tf_op jit(solution)/shard_map/all_to_all | solution.py:36
  34.5 40.3 %copy-start.1 = (bf16[16,4,2048]{2,1,0:T(4,128)(2,1)S(1)}, bf16[16,4,2048]{2,1,0:T(4,128)(2,1)}, u32[]{:S(2)}) copy-start(bf16[16,4,2048]{2,1,0:T(4,128)(2,1)} %hidden_ref.3) | copy-start | bytes 786436
  34.5 40.3 %copy-start.5 = (f32[2048]{0:T(1024)S(1)}, f32[2048]{0:T(1024)}, u32[]{:S(2)}) copy-start(f32[2048]{0:T(1024)} %param.24) | copy-start | bytes 24580
  34.5 40.3 %copy-start.6 = (f32[2048]{0:T(1024)S(1)}, f32[2048]{0:T(1024)}, u32[]{:S(2)}) copy-start(f32[2048]{0:T(1024)} %param.25) | copy-start | bytes 24580
  92.2 18.4 %copy-start.4 = (s32[2]{0:T(128)S(1)}, s32[2]{0:T(128)}, u32[]{:S(2)}) copy-start(s32[2]{0:T(128)} %copy-done.3) | copy-start | bytes 28
  92.2 18.4 %copy-start.7 = (f32[2048]{0:T(1024)S(1)}, f32[2048]{0:T(1024)}, u32[]{:S(2)}) copy-start(f32[2048]{0:T(1024)} %param.26) | copy-start | bytes 24580
